TPU v7x, 512 devices: a whole 4x4x16 slice. The times are simulated.
512 devices in a mesh: blk: 16 (over x_lo, y, core), chan: 32 (over z, x_hi).
Axes of the slice: x: 4 (x_hi: 2, x_lo: 2; x = x_hi * 2 + x_lo), y: 4, z: 16, core: 2. Of those that a mesh axis runs over, the one named last changes fastest.
Arguments:
- react_basis: bfloat16 [256, 2048, 128], P('blk', 'chan'), may hold values from -0.03125 to 0.03125
- prod_basis: bfloat16 [512, 2048, 128], P('blk', 'chan'), may hold values from -0.25 to 0.25
- react_radius: float32 [256], replicated, may hold values from 0.5 to 3
- prod_radius: float32 [512], replicated, may hold values from 0.5 to 3
- prod_weight: float32 [512], replicated, may hold values from 0.3 to 3
- angle_cos: float32 [128], replicated, may hold values from -1 to 1
- angle_weight: float32 [128], replicated, may hold values from 0.3 to 3
- coupling: int32 [32, 32], P('blk', 'chan'), may hold values 0 or 1
Outputs:
- kernel: float32 [2048, 2048], P('blk', 'chan')
All inputs are finite; a program needn't handle non-finite values. No bound on the sum of `coupling` on one device may be relied on, other than what follows from the above.
Results may differ from a plain program's by a relative error of at most 0.0029.
Values may be sent and summed in bfloat16 or wider, within the bound.
A program may use at most 64 MiB of HBM per device.

v0:
```python
import jax
import jax.numpy as jnp
from jax import lax
from jax.sharding import PartitionSpec as P

C = 2048
NTB = 32


wave_number = 480.0


def from_behind(shard, axis, by):
    peers = lax.axis_size(axis)
    return lax.ppermute(shard, axis, [(i, (i + by) % peers) for i in range(peers)])


def slab_integral(near, far, far_weight, angle_cos, angle_weight, basis_slab):
    near_e = near[:, None, None]
    far_e = far[None, :, None]
    dist = near_e * near_e + far_e * far_e - 2.0 * angle_cos[None, None, :] * near_e * far_e
    shifted = 1.0 + dist
    weight = (
        angle_weight[None, None, :]
        * far_weight[None, :, None]
        * jnp.cos(wave_number * jnp.sqrt(shifted))
        / shifted
    )
    return jnp.einsum(
        "rsg,scg->rcg",
        weight,
        basis_slab.astype(jnp.float32),
        precision=lax.Precision.HIGHEST,
        preferred_element_type=jnp.float32,
    )


def local(
    react_basis,
    prod_basis,
    react_radius,
    prod_radius,
    prod_weight,
    angle_cos,
    angle_weight,
    coupling,
):
    rows_here = react_basis.shape[0]
    slab_len = prod_basis.shape[0]
    index = lax.axis_index("blk")
    groups = lax.axis_size("blk")

    def radial_part(slab_id, count, source):
        return lax.dynamic_slice_in_dim(source, slab_id * count, count, 0)

    near = radial_part(index, rows_here, react_radius)

    def contribution(slab_id, basis_slab):
        far = radial_part(slab_id, slab_len, prod_radius)
        far_weight = radial_part(slab_id, slab_len, prod_weight)
        return slab_integral(near, far, far_weight, angle_cos, angle_weight, basis_slab)

    start_total = contribution(index, prod_basis)

    def cycle_step(step, carry):
        total, basis_slab = carry
        basis_slab = from_behind(basis_slab, "blk", 1)
        slab_id = jnp.mod(index - step, groups)
        return (total + contribution(slab_id, basis_slab), basis_slab)

    inner, unused_slab = lax.fori_loop(1, groups, cycle_step, (start_total, prod_basis))
    inner_b = inner.astype(jnp.bfloat16)
    terms = jnp.einsum(
        "rdg,rcg->dc",
        lax.all_gather(inner_b, "chan", axis=1, tiled=True),
        react_basis,
        preferred_element_type=jnp.float32,
    )
    full = lax.psum_scatter(terms, "blk", scatter_dimension=0, tiled=True)
    tile = C // NTB
    tiles_down = coupling.shape[0]
    tiles_across = coupling.shape[1]
    mask = jnp.broadcast_to(
        coupling.astype(jnp.float32)[:, None, :, None], (tiles_down, tile, tiles_across, tile)
    )
    mask = mask.reshape(tiles_down * tile, tiles_across * tile)
    return full * mask


def solution(mesh):
    return jax.shard_map(
        local,
        mesh=mesh,
        in_specs=(
            P("blk", "chan", None),
            P("blk", "chan", None),
            P(),
            P(),
            P(),
            P(),
            P(),
            P("blk", "chan"),
        ),
        out_specs=P("blk", "chan"),
        check_vma=False,
    )
```

profile of v0, /device:TPU:1, one launch (start us, length us, event | category | flops | bytes accessed | tf_op | source)
XLA Modules:
  0.0 592.9 jit_solution(10811176648007704008)
XLA Ops:
  15.5 302.1 %while.17 = (s32[]{:T(128)}, f32[16,64,128]{1,0,2:T(8,128)S(1)}, bf16[32,64,128]{2,1,0:T(8,128)(2,1)}, f32[128]{0:T(128)}, s32[]{:T(128)}, /*index=5*/f32[512]{0...) while((s32[]{:T(128)}, f32[16,64,128]{1,0,2:T(8,128)S(1)}, ...), condition=%wide.region_1.2_spmd, body=%wide.region_0.1_spmd.sunk | while | flops 50862768 | bytes 5823980 | solution.py:71
  15.5 4.6 collective-permute-start
  23.2 3.3 collective-permute-done
  28.2 5.1 fusion.31
  34.1 4.3 collective-permute-start
  41.4 4.8 collective-permute-done
  47.9 5.1 fusion.31
  53.7 2.8 collective-permute-start
  59.6 6.9 %collective-permute-done = bf16[32,64,128]{2,1,0:T(8,128)(2,1)S(1)} collective-permute-done((bf16[32,64,128]{2,1,0:T(8,128)(2,1)}, bf16[32,64,128]{2,1,0:T(8,128)(2,1)S(1)}, u32[]{:S(2)}, u32[]{:S(2)}) %collective-permute-start) | collective-permute-done | bytes 524320 | tf_op jit(solution)/shard_map/while/body/eval_jaxpr/ppermute | solution.py:15
  68.2 5.1 fusion.31
  74.0 1.9 collective-permute-start
  79.1 7.8 %collective-permute-done = bf16[32,64,128]{2,1,0:T(8,128)(2,1)S(1)} collective-permute-done((bf16[32,64,128]{2,1,0:T(8,128)(2,1)}, bf16[32,64,128]{2,1,0:T(8,128)(2,1)S(1)}, u32[]{:S(2)}, u32[]{:S(2)}) %collective-permute-start) | collective-permute-done | bytes 524320 | tf_op jit(solution)/shard_map/while/body/eval_jaxpr/ppermute | solution.py:15
  88.5 5.1 fusion.31
  94.3 1.9 collective-permute-start
  99.4 7.8 %collective-permute-done = bf16[32,64,128]{2,1,0:T(8,128)(2,1)S(1)} collective-permute-done((bf16[32,64,128]{2,1,0:T(8,128)(2,1)}, bf16[32,64,128]{2,1,0:T(8,128)(2,1)S(1)}, u32[]{:S(2)}, u32[]{:S(2)}) %collective-permute-start) | collective-permute-done | bytes 524320 | tf_op jit(solution)/shard_map/while/body/eval_jaxpr/ppermute | solution.py:15
  108.8 5.1 fusion.31
  114.6 1.9 collective-permute-start
  119.7 7.8 %collective-permute-done = bf16[32,64,128]{2,1,0:T(8,128)(2,1)S(1)} collective-permute-done((bf16[32,64,128]{2,1,0:T(8,128)(2,1)}, bf16[32,64,128]{2,1,0:T(8,128)(2,1)S(1)}, u32[]{:S(2)}, u32[]{:S(2)}) %collective-permute-start) | collective-permute-done | bytes 524320 | tf_op jit(solution)/shard_map/while/body/eval_jaxpr/ppermute | solution.py:15
  129.1 5.1 fusion.31
  134.9 1.9 collective-permute-start
  140.0 7.8 %collective-permute-done = bf16[32,64,128]{2,1,0:T(8,128)(2,1)S(1)} collective-permute-done((bf16[32,64,128]{2,1,0:T(8,128)(2,1)}, bf16[32,64,128]{2,1,0:T(8,128)(2,1)S(1)}, u32[]{:S(2)}, u32[]{:S(2)}) %collective-permute-start) | collective-permute-done | bytes 524320 | tf_op jit(solution)/shard_map/while/body/eval_jaxpr/ppermute | solution.py:15
  149.4 5.1 fusion.31
  155.2 1.9 collective-permute-start
  160.3 7.8 %collective-permute-done = bf16[32,64,128]{2,1,0:T(8,128)(2,1)S(1)} collective-permute-done((bf16[32,64,128]{2,1,0:T(8,128)(2,1)}, bf16[32,64,128]{2,1,0:T(8,128)(2,1)S(1)}, u32[]{:S(2)}, u32[]{:S(2)}) %collective-permute-start) | collective-permute-done | bytes 524320 | tf_op jit(solution)/shard_map/while/body/eval_jaxpr/ppermute | solution.py:15
  169.7 5.1 fusion.31
  175.5 1.9 collective-permute-start
  180.6 7.8 %collective-permute-done = bf16[32,64,128]{2,1,0:T(8,128)(2,1)S(1)} collective-permute-done((bf16[32,64,128]{2,1,0:T(8,128)(2,1)}, bf16[32,64,128]{2,1,0:T(8,128)(2,1)S(1)}, u32[]{:S(2)}, u32[]{:S(2)}) %collective-permute-start) | collective-permute-done | bytes 524320 | tf_op jit(solution)/shard_map/while/body/eval_jaxpr/ppermute | solution.py:15
  190.0 5.1 fusion.31
  195.9 1.9 collective-permute-start
  200.9 7.8 %collective-permute-done = bf16[32,64,128]{2,1,0:T(8,128)(2,1)S(1)} collective-permute-done((bf16[32,64,128]{2,1,0:T(8,128)(2,1)}, bf16[32,64,128]{2,1,0:T(8,128)(2,1)S(1)}, u32[]{:S(2)}, u32[]{:S(2)}) %collective-permute-start) | collective-permute-done | bytes 524320 | tf_op jit(solution)/shard_map/while/body/eval_jaxpr/ppermute | solution.py:15
  210.3 5.1 fusion.31
  216.2 1.9 collective-permute-start
  221.2 7.8 %collective-permute-done = bf16[32,64,128]{2,1,0:T(8,128)(2,1)S(1)} collective-permute-done((bf16[32,64,128]{2,1,0:T(8,128)(2,1)}, bf16[32,64,128]{2,1,0:T(8,128)(2,1)S(1)}, u32[]{:S(2)}, u32[]{:S(2)}) %collective-permute-start) | collective-permute-done | bytes 524320 | tf_op jit(solution)/shard_map/while/body/eval_jaxpr/ppermute | solution.py:15
  230.6 5.1 fusion.31
  236.5 1.9 collective-permute-start
  241.5 7.8 %collective-permute-done = bf16[32,64,128]{2,1,0:T(8,128)(2,1)S(1)} collective-permute-done((bf16[32,64,128]{2,1,0:T(8,128)(2,1)}, bf16[32,64,128]{2,1,0:T(8,128)(2,1)S(1)}, u32[]{:S(2)}, u32[]{:S(2)}) %collective-permute-start) | collective-permute-done | bytes 524320 | tf_op jit(solution)/shard_map/while/body/eval_jaxpr/ppermute | solution.py:15
  250.9 5.1 fusion.31
  256.8 1.9 collective-permute-start
  261.8 7.8 %collective-permute-done = bf16[32,64,128]{2,1,0:T(8,128)(2,1)S(1)} collective-permute-done((bf16[32,64,128]{2,1,0:T(8,128)(2,1)}, bf16[32,64,128]{2,1,0:T(8,128)(2,1)S(1)}, u32[]{:S(2)}, u32[]{:S(2)}) %collective-permute-start) | collective-permute-done | bytes 524320 | tf_op jit(solution)/shard_map/while/body/eval_jaxpr/ppermute | solution.py:15
  271.2 5.1 fusion.31
  277.1 1.9 collective-permute-start
  282.1 7.8 %collective-permute-done = bf16[32,64,128]{2,1,0:T(8,128)(2,1)S(1)} collective-permute-done((bf16[32,64,128]{2,1,0:T(8,128)(2,1)}, bf16[32,64,128]{2,1,0:T(8,128)(2,1)S(1)}, u32[]{:S(2)}, u32[]{:S(2)}) %collective-permute-start) | collective-permute-done | bytes 524320 | tf_op jit(solution)/shard_map/while/body/eval_jaxpr/ppermute | solution.py:15
  291.5 5.1 fusion.31
  302.4 7.8 %collective-permute-done = bf16[32,64,128]{2,1,0:T(8,128)(2,1)S(1)} collective-permute-done((bf16[32,64,128]{2,1,0:T(8,128)(2,1)}, bf16[32,64,128]{2,1,0:T(8,128)(2,1)S(1)}, u32[]{:S(2)}, u32[]{:S(2)}) %collective-permute-start) | collective-permute-done | bytes 524320 | tf_op jit(solution)/shard_map/while/body/eval_jaxpr/ppermute | solution.py:15
  311.8 5.1 fusion.31
  318.9 190.9 %all-gather.2.cloned.1.call-done = bf16[16,2048,128]{2,1,0:T(8,128)(2,1)} async-done(((bf16[16,64,128]{2,1,0:T(8,128)(2,1)}), bf16[16,2048,128]{2,1,0:T(8,128)(2,1)}) %all-gather.2.cloned.1.call-update) | async-done | bytes 8388624 | tf_op jit(solution)/shard_map/all_gather | solution.py:75
  509.7 6.8 %convolution_bitcast_fusion.1 = f32[2048,64]{0,1:T(8,128)} fusion(bf16[16,2048,128]{2,1,0:T(8,128)(2,1)} %all-gather.2.cloned.1.call-done, bf16[16,64,128]{2,1,0:T(8,128)(2,1)S(1)} %copy-done), kind=kOutput, calls=%fused_computation.22 | convolution fusion | flops 536870912 | bytes 9175040 | tf_op jit(solution)/shard_map/rdg,rcg->dc/dot_general | solution.py:73
  516.8 67.9 %reduce-scatter.2.cloned.1.call-done = f32[128,64]{0,1:T(8,128)} async-done(((f32[2048,64]{0,1:T(8,128)}), f32[128,64]{0,1:T(8,128)}) %reduce-scatter.2.cloned.1.call-update) | async-done | bytes 32784 | tf_op jit(solution)/shard_map/reduce_scatter | solution.py:79
  (149 shorter events, 95.7 us)
Async XLA Ops:
  6.5 503.2 %copy-start = (bf16[16,64,128]{2,1,0:T(8,128)(2,1)S(1)}, bf16[16,64,128]{2,1,0:T(8,128)(2,1)}, u32[]{:S(2)}) copy-start(bf16[16,64,128]{2,1,0:T(8,128)(2,1)} %param.10) | copy-start | bytes 786436
  6.5 503.2 %all-gather.2.cloned.1.call-start = ((), (), s32[]{:S(2)}) async-start(), calls=%async_computation.1 | async-start | bytes 8650752 | tf_op jit(solution)/shard_map/all_gather | solution.py:75
  7.6 5.3 copy-start.1
  15.5 11.0 %collective-permute-start = (bf16[32,64,128]{2,1,0:T(8,128)(2,1)}, bf16[32,64,128]{2,1,0:T(8,128)(2,1)S(1)}, u32[]{:S(2)}, u32[]{:S(2)}) collective-permute-start(bf16[32,64,128]{2,1,0:T(8,128)(2,1)} %get-tuple-element.352), channel_id=1, source_target_pairs={{0,32},{32,64},{64,96},{96,128},{128,160},{160,192},{192,224},{224... | collective-permute-start | bytes 1572872 | tf_op jit(solution)/shard_map/while/body/eval_jaxpr/ppermute | solution.py:15
  34.1 12.2 %collective-permute-start = (bf16[32,64,128]{2,1,0:T(8,128)(2,1)}, bf16[32,64,128]{2,1,0:T(8,128)(2,1)S(1)}, u32[]{:S(2)}, u32[]{:S(2)}) collective-permute-start(bf16[32,64,128]{2,1,0:T(8,128)(2,1)} %get-tuple-element.352), channel_id=1, source_target_pairs={{0,32},{32,64},{64,96},{96,128},{128,160},{160,192},{192,224},{224... | collective-permute-start | bytes 1572872 | tf_op jit(solution)/shard_map/while/body/eval_jaxpr/ppermute | solution.py:15
  53.7 12.8 %collective-permute-start = (bf16[32,64,128]{2,1,0:T(8,128)(2,1)}, bf16[32,64,128]{2,1,0:T(8,128)(2,1)S(1)}, u32[]{:S(2)}, u32[]{:S(2)}) collective-permute-start(bf16[32,64,128]{2,1,0:T(8,128)(2,1)} %get-tuple-element.352), channel_id=1, source_target_pairs={{0,32},{32,64},{64,96},{96,128},{128,160},{160,192},{192,224},{224... | collective-permute-start | bytes 1572872 | tf_op jit(solution)/shard_map/while/body/eval_jaxpr/ppermute | solution.py:15
  74.0 12.8 %collective-permute-start = (bf16[32,64,128]{2,1,0:T(8,128)(2,1)}, bf16[32,64,128]{2,1,0:T(8,128)(2,1)S(1)}, u32[]{:S(2)}, u32[]{:S(2)}) collective-permute-start(bf16[32,64,128]{2,1,0:T(8,128)(2,1)} %get-tuple-element.352), channel_id=1, source_target_pairs={{0,32},{32,64},{64,96},{96,128},{128,160},{160,192},{192,224},{224... | collective-permute-start | bytes 1572872 | tf_op jit(solution)/shard_map/while/body/eval_jaxpr/ppermute | solution.py:15
  94.3 12.8 %collective-permute-start = (bf16[32,64,128]{2,1,0:T(8,128)(2,1)}, bf16[32,64,128]{2,1,0:T(8,128)(2,1)S(1)}, u32[]{:S(2)}, u32[]{:S(2)}) collective-permute-start(bf16[32,64,128]{2,1,0:T(8,128)(2,1)} %get-tuple-element.352), channel_id=1, source_target_pairs={{0,32},{32,64},{64,96},{96,128},{128,160},{160,192},{192,224},{224... | collective-permute-start | bytes 1572872 | tf_op jit(solution)/shard_map/while/body/eval_jaxpr/ppermute | solution.py:15
  114.6 12.8 %collective-permute-start = (bf16[32,64,128]{2,1,0:T(8,128)(2,1)}, bf16[32,64,128]{2,1,0:T(8,128)(2,1)S(1)}, u32[]{:S(2)}, u32[]{:S(2)}) collective-permute-start(bf16[32,64,128]{2,1,0:T(8,128)(2,1)} %get-tuple-element.352), channel_id=1, source_target_pairs={{0,32},{32,64},{64,96},{96,128},{128,160},{160,192},{192,224},{224... | collective-permute-start | bytes 1572872 | tf_op jit(solution)/shard_map/while/body/eval_jaxpr/ppermute | solution.py:15
  134.9 12.8 %collective-permute-start = (bf16[32,64,128]{2,1,0:T(8,128)(2,1)}, bf16[32,64,128]{2,1,0:T(8,128)(2,1)S(1)}, u32[]{:S(2)}, u32[]{:S(2)}) collective-permute-start(bf16[32,64,128]{2,1,0:T(8,128)(2,1)} %get-tuple-element.352), channel_id=1, source_target_pairs={{0,32},{32,64},{64,96},{96,128},{128,160},{160,192},{192,224},{224... | collective-permute-start | bytes 1572872 | tf_op jit(solution)/shard_map/while/body/eval_jaxpr/ppermute | solution.py:15
  155.2 12.8 %collective-permute-start = (bf16[32,64,128]{2,1,0:T(8,128)(2,1)}, bf16[32,64,128]{2,1,0:T(8,128)(2,1)S(1)}, u32[]{:S(2)}, u32[]{:S(2)}) collective-permute-start(bf16[32,64,128]{2,1,0:T(8,128)(2,1)} %get-tuple-element.352), channel_id=1, source_target_pairs={{0,32},{32,64},{64,96},{96,128},{128,160},{160,192},{192,224},{224... | collective-permute-start | bytes 1572872 | tf_op jit(solution)/shard_map/while/body/eval_jaxpr/ppermute | solution.py:15
  175.5 12.8 %collective-permute-start = (bf16[32,64,128]{2,1,0:T(8,128)(2,1)}, bf16[32,64,128]{2,1,0:T(8,128)(2,1)S(1)}, u32[]{:S(2)}, u32[]{:S(2)}) collective-permute-start(bf16[32,64,128]{2,1,0:T(8,128)(2,1)} %get-tuple-element.352), channel_id=1, source_target_pairs={{0,32},{32,64},{64,96},{96,128},{128,160},{160,192},{192,224},{224... | collective-permute-start | bytes 1572872 | tf_op jit(solution)/shard_map/while/body/eval_jaxpr/ppermute | solution.py:15
  195.9 12.8 %collective-permute-start = (bf16[32,64,128]{2,1,0:T(8,128)(2,1)}, bf16[32,64,128]{2,1,0:T(8,128)(2,1)S(1)}, u32[]{:S(2)}, u32[]{:S(2)}) collective-permute-start(bf16[32,64,128]{2,1,0:T(8,128)(2,1)} %get-tuple-element.352), channel_id=1, source_target_pairs={{0,32},{32,64},{64,96},{96,128},{128,160},{160,192},{192,224},{224... | collective-permute-start | bytes 1572872 | tf_op jit(solution)/shard_map/while/body/eval_jaxpr/ppermute | solution.py:15
  216.2 12.8 %collective-permute-start = (bf16[32,64,128]{2,1,0:T(8,128)(2,1)}, bf16[32,64,128]{2,1,0:T(8,128)(2,1)S(1)}, u32[]{:S(2)}, u32[]{:S(2)}) collective-permute-start(bf16[32,64,128]{2,1,0:T(8,128)(2,1)} %get-tuple-element.352), channel_id=1, source_target_pairs={{0,32},{32,64},{64,96},{96,128},{128,160},{160,192},{192,224},{224... | collective-permute-start | bytes 1572872 | tf_op jit(solution)/shard_map/while/body/eval_jaxpr/ppermute | solution.py:15
  236.5 12.8 %collective-permute-start = (bf16[32,64,128]{2,1,0:T(8,128)(2,1)}, bf16[32,64,128]{2,1,0:T(8,128)(2,1)S(1)}, u32[]{:S(2)}, u32[]{:S(2)}) collective-permute-start(bf16[32,64,128]{2,1,0:T(8,128)(2,1)} %get-tuple-element.352), channel_id=1, source_target_pairs={{0,32},{32,64},{64,96},{96,128},{128,160},{160,192},{192,224},{224... | collective-permute-start | bytes 1572872 | tf_op jit(solution)/shard_map/while/body/eval_jaxpr/ppermute | solution.py:15
  256.8 12.8 %collective-permute-start = (bf16[32,64,128]{2,1,0:T(8,128)(2,1)}, bf16[32,64,128]{2,1,0:T(8,128)(2,1)S(1)}, u32[]{:S(2)}, u32[]{:S(2)}) collective-permute-start(bf16[32,64,128]{2,1,0:T(8,128)(2,1)} %get-tuple-element.352), channel_id=1, source_target_pairs={{0,32},{32,64},{64,96},{96,128},{128,160},{160,192},{192,224},{224... | collective-permute-start | bytes 1572872 | tf_op jit(solution)/shard_map/while/body/eval_jaxpr/ppermute | solution.py:15
  277.1 12.8 %collective-permute-start = (bf16[32,64,128]{2,1,0:T(8,128)(2,1)}, bf16[32,64,128]{2,1,0:T(8,128)(2,1)S(1)}, u32[]{:S(2)}, u32[]{:S(2)}) collective-permute-start(bf16[32,64,128]{2,1,0:T(8,128)(2,1)} %get-tuple-element.352), channel_id=1, source_target_pairs={{0,32},{32,64},{64,96},{96,128},{128,160},{160,192},{192,224},{224... | collective-permute-start | bytes 1572872 | tf_op jit(solution)/shard_map/while/body/eval_jaxpr/ppermute | solution.py:15
  297.4 12.8 %collective-permute-start = (bf16[32,64,128]{2,1,0:T(8,128)(2,1)}, bf16[32,64,128]{2,1,0:T(8,128)(2,1)S(1)}, u32[]{:S(2)}, u32[]{:S(2)}) collective-permute-start(bf16[32,64,128]{2,1,0:T(8,128)(2,1)} %get-tuple-element.352), channel_id=1, source_target_pairs={{0,32},{32,64},{64,96},{96,128},{128,160},{160,192},{192,224},{224... | collective-permute-start | bytes 1572872 | tf_op jit(solution)/shard_map/while/body/eval_jaxpr/ppermute | solution.py:15
  317.7 198.9 %copy-start.2 = (s32[2,1]{0,1:T(1,128)S(1)}, s32[2,1]{0,1:T(1,128)}, u32[]{:S(2)}) copy-start(s32[2,1]{0,1:T(1,128)} %param.17) | copy-start | bytes 28
  318.8 265.9 %reduce-scatter.2.cloned.1.call-start = ((), (), s32[]{:S(2)}) async-start(), calls=%async_computation.2 | async-start | bytes 557056 | tf_op jit(solution)/shard_map/reduce_scatter | solution.py:79
Sparse Core Ops, SparseCore 0:
  318.9 190.7 all-gather.1
  516.7 67.9 reduce-scatter.1
where the time goes:
time: 596 us; the launch traced here: 593 us
  waiting for transfers between devices  367 us (62%)
  matrix products  83.7 us (14%)
  local copies, waits for them, and re-layouts  52.8 us (9%)
  other arithmetic  40 us (7%)
  starting transfers between devices  34.6 us (6%)
  between operations  13.5 us (2%)
    all_gather x1, waiting for transfers between devices, local(): lax.all_gather(inner_b, 'chan', axis=1, tiled=True)  191 us
    ppermute x15, waiting for transfers between devices, from_behind(): lax.ppermute(shard, axis, [(i, (i + by) % peers) for i in range(peers)])  109 us
    dot_general x16, matrix products, slab_integral(): jnp.einsum('rsg,scg->rcg', weight, basis_slab.astype(jnp.float32), precis...  76.9 us
    reduce_scatter x1, waiting for transfers between devices, local(): full = lax.psum_scatter(terms, 'blk', scatter_dimension=0, tiled=True)  67.9 us
    ppermute x15, starting transfers between devices, from_behind(): lax.ppermute(shard, axis, [(i, (i + by) % peers) for i in range(peers)])  34.5 us
    ppermute x15, local copies, waits for them, and re-layouts, from_behind(): lax.ppermute(shard, axis, [(i, (i + by) % peers) for i in range(peers)])  24.4 us
    mul x16, other arithmetic, slab_integral(): far_e * far_e  12.2 us
    dynamic_slice x16, local copies, waits for them, and re-layouts, radial_part(): return lax.dynamic_slice_in_dim(source, slab_id * count, count, 0)  12.1 us
  transfers between devices with their start and end apart: 17, of which 17 were waited for; matrix products, arithmetic and copies ran while one was open for 8% of the time, Pallas kernels for 0%

commit v1 on v0

v1 whole, which is shorter than its diff:
```python
import jax
import jax.numpy as jnp
from jax import lax
from jax.experimental import pallas as pl
from jax.experimental.pallas import tpu as pltpu
from jax.sharding import PartitionSpec as P

MESH = pl.DeviceIdType.MESH
F32 = jnp.float32
BF16 = jnp.bfloat16

turns_per_unit = 76.39437268410976
cos_terms = (
    0.9999999890590228,
    -19.739204499454026,
    64.93911745990036,
    -85.45013953095037,
    60.16763095136588,
    -25.96759924965491,
    6.528658162567069,
)
y_order = (2, 1, 3, 0)


def lanes(a, b):
    return jnp.concatenate([a, b], axis=1)


def kernel(
    pr_ref,
    pw_ref,
    rr_ref,
    cos_ref,
    aw_ref,
    r_ref,
    p_ref,
    o_ref,
    s_r,
    s_p,
    pr_t,
    pw_t,
    r_send,
    p_send,
    r_got,
    p_got,
    weight,
    in_send,
    in_got,
    r_row,
    in_row,
    rhs,
    y_send,
    y_got,
    own,
    z_send,
    z_got,
    rb_ss,
    rb_rs,
    pb_ss,
    pb_rs,
    rz_ss,
    rz_rs,
    iz_ss,
    iz_rs,
    rr_ss,
    rr_rs,
    ir_ss,
    ir_rs,
    y_ss,
    y_rs,
    z_ss,
    z_rs,
):
    b = lax.axis_index("blk")
    h = lax.axis_index("chan")
    z, xh = h // 2, h % 2
    xl, y, co = b // 8, (b // 2) % 4, b % 2
    quad = xl * 2 + co

    def at_blk(off):
        return ((b + off) % 16, h)

    def at_z(off):
        return (b, ((z + off) % 16) * 2 + xh)

    def remote(src, dst, ss, rs, dev):
        return pltpu.make_async_remote_copy(
            src_ref=src, dst_ref=dst, send_sem=ss, recv_sem=rs, device_id=dev, device_id_type=MESH
        )

    def row_peer(off):
        j = (xh * 4 + quad + off) % 8
        return j, (((j // 2) % 2) * 8 + y * 2 + j % 2, z * 2 + j // 4)

    barrier = pltpu.get_barrier_semaphore()

    @pl.loop(1, 16)
    def _(off):
        pl.semaphore_signal(barrier, inc=1, device_id=at_blk(off), device_id_type=MESH)
        pl.semaphore_signal(barrier, inc=1, device_id=at_z(off), device_id_type=MESH)

    @pl.loop(0, 4)
    def _(i):
        dev = ((i // 2) * 8 + y * 2 + i % 2, z * 2 + 1 - xh)
        pl.semaphore_signal(barrier, inc=1, device_id=dev, device_id_type=MESH)

    @pl.loop(0, 8)
    def _(i):
        t = r_ref[pl.ds(2 * i, 2)].reshape(128, 128).astype(F32).T
        lo, hi = t[:64], t[64:]
        s_r[pl.ds(2 * i, 64, stride=16), :] = lanes(lo[:, :64], hi[:, :64])
        s_r[pl.ds(2 * i + 1, 64, stride=16), :] = lanes(lo[:, 64:], hi[:, 64:])

    @pl.loop(0, 16)
    def _(d):
        r_send[d] = s_r[pl.ds(pl.multiple_of(64 * d, 64), 64), :].astype(BF16)

    pl.semaphore_wait(barrier, 34)

    @pl.loop(1, 16)
    def _(off):
        d = (b + off) % 16
        remote(r_send.at[d], r_got.at[b], rb_ss.at[off], rb_rs.at[b], at_blk(off)).start()

    r_got[b] = r_send[b]

    @pl.loop(0, 16)
    def _(i):
        x = jnp.concatenate([p_ref[i], p_ref[16 + i]], axis=0)
        s_p[pl.ds(i, 128, stride=16), :] = x.astype(F32).T

    @pl.loop(0, 16)
    def _(off):
        d = (b + off) % 16
        for gh in range(2):
            start = pl.multiple_of(gh * 1024 + 64 * d, 64)
            p_send[d, gh] = s_p[pl.ds(start, 64), :].astype(BF16)

        @pl.when(off > 0)
        def _():
            remote(p_send.at[d], p_got.at[b], pb_ss.at[off], pb_rs.at[b], at_blk(off)).start()

    p_got[b] = p_send[b]

    for k in range(4):
        cols = slice(128 * k, 128 * k + 128)
        pr_t[cols, :] = jnp.broadcast_to(pr_ref[:, cols], (128, 128)).T
        pw_t[cols, :] = jnp.broadcast_to(pw_ref[:, cols], (128, 128)).T

    def make_weight(gi):
        g = (gi % 2) * 64 + 4 * b + gi // 2
        two_cos = 2.0 * cos_ref[g]
        ang = aw_ref[g]

        @pl.loop(0, 16)
        def _(src):
            for sh in range(2):
                rows = pl.ds(pl.multiple_of(src * 32 + sh * 16, 16), 16)
                far = pr_t[rows, :]
                scale = pw_t[rows, :] * ang
                far2 = far * far
                for half in range(2):
                    cols = slice(128 * half, 128 * half + 128)
                    near = rr_ref[:, cols]
                    q = (1.0 + near * near) + far2 - (two_cos * near) * far
                    rs = lax.rsqrt(q)
                    root = q * rs
                    root = root + (0.5 * rs) * (q - root * root)
                    turns = root * turns_per_unit
                    f = turns - jnp.round(turns)
                    u = f * f
                    c = jnp.full_like(u, cos_terms[6])
                    for term in cos_terms[5::-1]:
                        c = c * u + term
                    w = scale * c * (rs * rs)
                    w_hi = w.astype(BF16)
                    w_lo = (w - w_hi.astype(F32)).astype(BF16)
                    at = pl.multiple_of(sh * 256 + src * 16, 16)
                    weight[gi, pl.ds(at, 16), cols] = w_hi
                    weight[gi, pl.ds(at + 512, 16), cols] = w_lo

    @pl.loop(0, 4)
    def _(gi):
        make_weight(gi)

    @pl.loop(0, 4)
    def _(t):
        qd = (b // 4 + t) % 4

        @pl.loop(0, 4)
        def _(i):
            src = qd * 4 + i

            @pl.when(src != b)
            def _():
                remote(r_send.at[0], r_got.at[src], rb_ss.at[0], rb_rs.at[src], at_blk(1)).wait_recv()

        @pl.loop(0, 4)
        def _(jj):
            j = (z // 4 + 2 + jj) % 4
            k = j * 4 + qd
            block = r_got.at[pl.ds(qd * 4, 4), pl.ds(pl.multiple_of(16 * j, 16), 16), :]

            @pl.when(k != z)
            def _():
                remote(block, r_row.at[quad, z], rz_ss.at[k], rz_rs.at[z], (b, k * 2 + xh)).start()

            @pl.when(k == z)
            def _():
                r_row[quad, z] = block[...]

    @pl.loop(4, 8)
    def _(gi):
        make_weight(gi)

    @pl.loop(1, 16)
    def _(off):
        src = (b + off) % 16
        remote(p_send.at[0], p_got.at[src], pb_ss.at[0], pb_rs.at[src], at_blk(1)).wait_recv()

    @pl.loop(0, 4)
    def _(t):
        j = (z // 4 + 2 + t) % 4
        parts = []
        for gh in range(2):
            x = p_got[:, gh, pl.ds(pl.multiple_of(16 * j, 16), 16), :].reshape(256, 128)
            xt = x.T
            lhs = jnp.concatenate([xt[:64], xt[64:], xt[:64], xt[64:]], axis=1)
            parts.append(jnp.dot(lhs, weight[j * 2 + gh], preferred_element_type=F32))
        for qd in range(4):
            cols = slice(64 * qd, 64 * qd + 64)
            in_send[j * 4 + qd] = lanes(parts[0][:, cols], parts[1][:, cols]).astype(BF16)

        @pl.loop(0, 4)
        def _(qd):
            k = j * 4 + qd

            @pl.when(k != z)
            def _():
                remote(in_send.at[k], in_got.at[z], iz_ss.at[k], iz_rs.at[z], (b, k * 2 + xh)).start()

            @pl.when(k == z)
            def _():
                in_got[z] = in_send[z]

    @pl.loop(1, 16)
    def _(off):
        src = (z + off) % 16
        remote(r_row.at[0, 0], r_row.at[quad, src], rz_ss.at[0], rz_rs.at[src], at_z(1)).wait_recv()

    def quad_peer(off):
        q = (quad + off) % 4
        return q, ((q // 2) * 8 + y * 2 + q % 2, h)

    @pl.loop(1, 4)
    def _(off):
        _, dev = quad_peer(off)
        remote(r_row.at[quad], r_row.at[quad], rr_ss.at[off], rr_rs.at[quad], dev).start()

    me = xh * 4 + quad
    for t in range(4):
        yt = (y + y_order[t]) % 4

        @pl.loop(0, 4)
        def _(i):
            src = (i // 2) * 8 + yt * 2 + i % 2

            @pl.when(src != z)
            def _():
                remote(in_send.at[0], in_got.at[src], iz_ss.at[0], iz_rs.at[src], at_z(1)).wait_recv()

        rows = pl.ds(pl.multiple_of(xh * 64, 64), 64)
        cols = pl.ds(pl.multiple_of(quad * 128, 128), 128)

        @pl.loop(1, 8)
        def _(off):
            j, dev = row_peer(off)
            src = ((j // 2) % 2) * 8 + yt * 2 + j % 2
            remote(in_got.at[src], in_row.at[t, rows, cols], ir_ss.at[t, off], ir_rs.at[t, me], dev).start()

        in_row[t, rows, cols] = in_got[xl * 8 + yt * 2 + co]

    @pl.loop(1, 4)
    def _(off):
        q, dev = quad_peer(off)
        remote(r_row.at[0], r_row.at[q], rr_ss.at[0], rr_rs.at[q], dev).wait_recv()

    @pl.loop(0, 4)
    def _(q):
        for n in range(8):
            x0 = r_row[q, 2 * n].reshape(64, 128)
            x1 = r_row[q, 2 * n + 1].reshape(64, 128)
            at = pl.multiple_of(q * 128, 128)
            cols = slice(128 * n, 128 * n + 128)
            rhs[pl.ds(at, 64), cols] = lanes(x0[:, :64], x1[:, :64])
            rhs[pl.ds(at + 64, 64), cols] = lanes(x0[:, 64:], x1[:, 64:])

    for t in range(4):

        @pl.loop(1, 8)
        def _(off):
            j, dev = row_peer(off)
            src_rows = pl.ds(pl.multiple_of((j // 4) * 64, 64), 64)
            src_cols = pl.ds(pl.multiple_of((j % 4) * 128, 128), 128)
            remote(
                in_got.at[0], in_row.at[t, src_rows, src_cols], ir_ss.at[0, 0], ir_rs.at[t, j], dev
            ).wait_recv()

        @pl.loop(0, 4)
        def _(n):
            cols = pl.ds(pl.multiple_of(n * 256, 256), 256)
            part = jnp.dot(in_row[t], rhs[:, cols], preferred_element_type=F32)
            if t < 3:
                y_send[t, :, cols] = part.astype(BF16)
            else:
                own[:, cols] = part

        if t < 3:
            yt = (y + y_order[t]) % 4
            dev = (xl * 8 + yt * 2 + co, h)
            remote(y_send.at[t], y_got.at[t], y_ss.at[t], y_rs.at[t], dev).start()

    for t in range(3):
        dev = (xl * 8 + ((y + y_order[t]) % 4) * 2 + co, h)
        remote(y_send.at[t], y_got.at[t], y_ss.at[t], y_rs.at[t], dev).wait_recv()

    @pl.loop(0, 8)
    def _(i):
        n = (z // 2 + 4 + i) % 8
        cols = pl.ds(pl.multiple_of(n * 128, 128), 128)
        s = own[:, cols]
        for t in range(3):
            s = s + y_got[t, :, cols].astype(F32)
        top, low = s[:64], s[64:]
        z_send[2 * n] = lanes(top[:, :64], low[:, :64]).astype(BF16)
        z_send[2 * n + 1] = lanes(top[:, 64:], low[:, 64:]).astype(BF16)

        @pl.loop(0, 2)
        def _(e):
            k = 2 * n + e

            @pl.when(k != z)
            def _():
                remote(z_send.at[k], z_got.at[z], z_ss.at[k], z_rs.at[z], (b, k * 2 + xh)).start()

            @pl.when(k == z)
            def _():
                z_got[z] = z_send[z]

    @pl.loop(1, 16)
    def _(off):
        src = (z + off) % 16
        remote(z_send.at[0], z_got.at[src], z_ss.at[0], z_rs.at[src], at_z(1)).wait_recv()

    total = z_got[0].astype(F32)
    for k in range(1, 16):
        total = total + z_got[k].astype(F32)
    o_ref[:64, :] = total[:, :64]
    o_ref[64:, :] = total[:, 64:]

    @pl.loop(1, 16)
    def _(off):
        k = (z + off) % 16
        remote(r_send.at[0], r_got.at[0], rb_ss.at[off], rb_rs.at[0], at_blk(1)).wait_send()
        remote(p_send.at[0], p_got.at[0], pb_ss.at[off], pb_rs.at[0], at_blk(1)).wait_send()
        remote(r_got.at[pl.ds(0, 4), pl.ds(0, 16), :], r_row.at[0, 0], rz_ss.at[k], rz_rs.at[0], at_z(1)).wait_send()
        remote(in_send.at[0], in_got.at[0], iz_ss.at[k], iz_rs.at[0], at_z(1)).wait_send()
        remote(z_send.at[0], z_got.at[0], z_ss.at[k], z_rs.at[0], at_z(1)).wait_send()

    @pl.loop(1, 4)
    def _(off):
        remote(r_row.at[0], r_row.at[0], rr_ss.at[off], rr_rs.at[0], at_blk(1)).wait_send()

    for t in range(4):

        @pl.loop(1, 8)
        def _(off):
            remote(in_got.at[0], in_got.at[0], ir_ss.at[t, off], ir_rs.at[t, 0], at_blk(1)).wait_send()

        if t < 3:
            remote(y_send.at[t], y_got.at[t], y_ss.at[t], y_rs.at[t], at_blk(1)).wait_send()


def local(react_basis, prod_basis, react_radius, prod_radius, prod_weight, angle_cos, angle_weight, coupling):
    dma = pltpu.SemaphoreType.DMA
    vmem = pl.BlockSpec(memory_space=pltpu.VMEM)
    smem = pl.BlockSpec(memory_space=pltpu.SMEM)
    full = pl.pallas_call(
        kernel,
        out_shape=jax.ShapeDtypeStruct((128, 64), F32),
        in_specs=[vmem, vmem, vmem, smem, smem, vmem, vmem],
        out_specs=vmem,
        scratch_shapes=[
            pltpu.VMEM((1024, 128), F32),
            pltpu.VMEM((2048, 128), F32),
            pltpu.VMEM((512, 128), F32),
            pltpu.VMEM((512, 128), F32),
            pltpu.VMEM((16, 64, 128), BF16),
            pltpu.VMEM((16, 2, 64, 128), BF16),
            pltpu.VMEM((16, 64, 128), BF16),
            pltpu.VMEM((16, 2, 64, 128), BF16),
            pltpu.VMEM((8, 1024, 256), BF16),
            pltpu.VMEM((16, 64, 128), BF16),
            pltpu.VMEM((16, 64, 128), BF16),
            pltpu.VMEM((4, 16, 4, 16, 128), BF16),
            pltpu.VMEM((4, 128, 512), BF16),
            pltpu.VMEM((512, 1024), BF16),
            pltpu.VMEM((3, 128, 1024), BF16),
            pltpu.VMEM((3, 128, 1024), BF16),
            pltpu.VMEM((128, 1024), F32),
            pltpu.VMEM((16, 64, 128), BF16),
            pltpu.VMEM((16, 64, 128), BF16),
            dma((16,)),
            dma((16,)),
            dma((16,)),
            dma((16,)),
            dma((16,)),
            dma((16,)),
            dma((16,)),
            dma((16,)),
            dma((4,)),
            dma((4,)),
            dma((4, 8)),
            dma((4, 8)),
            dma((3,)),
            dma((3,)),
            dma((16,)),
            dma((16,)),
        ],
        compiler_params=pltpu.CompilerParams(
            collective_id=0, has_side_effects=True, vmem_limit_bytes=48 * 2**20
        ),
        cost_estimate=pl.CostEstimate(flops=10**9, bytes_accessed=10**6, transcendentals=10**6),
    )(
        prod_radius.reshape(1, -1),
        prod_weight.reshape(1, -1),
        react_radius.reshape(1, -1),
        angle_cos,
        angle_weight,
        react_basis,
        prod_basis,
    )
    mask = jnp.repeat(coupling.astype(F32), 64, axis=0)
    return full * mask


def solution(mesh):
    return jax.shard_map(
        local,
        mesh=mesh,
        in_specs=(P("blk", "chan", None), P("blk", "chan", None), P(), P(), P(), P(), P(), P("blk", "chan")),
        out_specs=P("blk", "chan"),
        check_vma=False,
    )
```

time: 596 us -> 93.2 us (0.16)
  the two profiles are of different devices: /device:TPU:1 before, /device:TPU:8 now
where the time goes in v1:
time: 93.2 us; the launch traced here: 93 us
  Pallas kernels  88.8 us (95%)
  local copies, waits for them, and re-layouts  4.1 us (4%)
    pallas_call x1, Pallas kernels, local(): pl.pallas_call(kernel, out_shape=jax.ShapeDtypeStruct((128, 64), F32), in...  88.8 us
    unnamed x16, local copies, waits for them, and re-layouts  3.25 us

profile of v1, /device:TPU:8, one launch (start us, length us, event | category | flops | bytes accessed | tf_op | source)
XLA Modules:
  0.0 93.0 jit_solution(663932509357506415)
XLA Ops:
  0.0 0.0 copy-start.7
  0.0 0.0 copy-start.6
  0.0 0.7 copy-done.7
  0.7 0.0 copy-start.3
  0.7 0.0 copy-start.2
  0.7 0.1 broadcast_in_dim.5
  0.7 0.0 copy-start.4
  0.7 0.0 copy-start.5
  0.7 0.1 broadcast_in_dim.6
  0.8 0.0 copy-done.6
  0.8 0.5 copy-done.3
  1.3 0.0 copy-done.2
  1.4 0.1 copy-done.4
  1.4 0.0 copy-done.5
  1.4 0.0 copy-start
  1.4 1.0 %copy-done = bf16[32,64,128]{2,1,0:T(8,128)(2,1)S(1)} copy-done((bf16[32,64,128]{2,1,0:T(8,128)(2,1)S(1)}, bf16[32,64,128]{2,1,0:T(8,128)(2,1)}, u32[]{:S(2)}) %copy-start) | copy-done | bytes 524312
  2.5 0.0 copy-start.1
  2.5 0.9 %copy-done.1 = bf16[16,64,128]{2,1,0:T(8,128)(2,1)S(1)} copy-done((bf16[16,64,128]{2,1,0:T(8,128)(2,1)S(1)}, bf16[16,64,128]{2,1,0:T(8,128)(2,1)}, u32[]{:S(2)}) %copy-start.1) | copy-done | bytes 262168
  3.4 88.8 %shard_map.82 = f32[128,64]{1,0:T(8,128)S(1)} custom-call(f32[1,512]{1,0:T(1,128)S(1)} %bitcast.5, f32[1,512]{1,0:T(1,128)S(1)} %bitcast.6, f32[1,256]{1,0:T(1,128)S(1)} %bitcast.7, f32[128]{0:T(128)S(1)} %copy-done.5, f32[128]{0:T(128)S(1)} %copy-done.6, bf16[16,64,128]{2,1,0:T(8,128)(2,1)S(1)} %copy-done.1, bf16[32,64,128]{2,1,0:T(8,128)(2,1)S(1)} %copy-done), custom_call_target="tpu_custom_call" | custom-call | flops 1000000000 | bytes 1000000 | tf_op jit(solution)/shard_map/pallas_call | solution.py:388
  92.2 0.1 broadcast_multiply_fusion
  92.3 0.7 copy.11
  (1 shorter events, 0.0 us)
Async XLA Ops:
  0.0 0.7 copy-start.7
  0.0 0.8 copy-start.6
  0.7 0.7 copy-start.3
  0.7 0.7 copy-start.2
  0.7 0.7 copy-start.4
  0.7 0.7 copy-start.5
  1.4 1.0 %copy-start = (bf16[32,64,128]{2,1,0:T(8,128)(2,1)S(1)}, bf16[32,64,128]{2,1,0:T(8,128)(2,1)}, u32[]{:S(2)}) copy-start(bf16[32,64,128]{2,1,0:T(8,128)(2,1)} %p_ref.1) | copy-start | bytes 1572868
  2.5 0.9 %copy-start.1 = (bf16[16,64,128]{2,1,0:T(8,128)(2,1)S(1)}, bf16[16,64,128]{2,1,0:T(8,128)(2,1)}, u32[]{:S(2)}) copy-start(bf16[16,64,128]{2,1,0:T(8,128)(2,1)} %r_ref.1) | copy-start | bytes 786436

commit v2 on v1

v2 whole, which is shorter than its diff:
```python
import jax
import jax.numpy as jnp
from jax import lax
from jax.experimental import pallas as pl
from jax.experimental.pallas import tpu as pltpu
from jax.sharding import PartitionSpec as P

MESH = pl.DeviceIdType.MESH
F32 = jnp.float32
BF16 = jnp.bfloat16

turns_per_unit = 76.39437268410976
cos_terms = (
    0.9999999890590228,
    -19.739204499454026,
    64.93911745990036,
    -85.45013953095037,
    60.16763095136588,
    -25.96759924965491,
    6.528658162567069,
)
y_order = (2, 1, 3)


def lanes(a, b):
    return jnp.concatenate([a, b], axis=1)


def kernel(
    pr_any,
    pw_any,
    rr_any,
    cos_any,
    aw_any,
    cp_any,
    r_any,
    p_any,
    o_ref,
    pr_ref,
    pw_ref,
    rr_ref,
    cos_ref,
    aw_ref,
    cp_ref,
    r_ref,
    p_ref,
    s_r,
    s_p,
    pr_t,
    pw_t,
    rr_t,
    near_t,
    rz_send,
    rz_got,
    rb_send,
    rb_got,
    r_row,
    rhs,
    p_send,
    p_got,
    weight,
    in_send,
    in_got,
    in_row,
    y_send,
    y_got,
    own,
    z_send,
    z_got,
    in_sem,
    rz_ss,
    rz_rs,
    rb_ss,
    rb_rs,
    rr_ss,
    rr_rs,
    pb_ss,
    pb_rs,
    iz_ss,
    iz_rs,
    ir_ss,
    ir_rs,
    y_ss,
    y_rs,
    z_ss,
    z_rs,
):
    b = lax.axis_index("blk")
    h = lax.axis_index("chan")
    z, xh = h // 2, h % 2
    xl, y, co = b // 8, (b // 2) % 4, b % 2
    quad = xl * 2 + co
    me = xh * 4 + quad

    def at_blk(off):
        return ((b + off) % 16, h)

    def at_z(off):
        return (b, ((z + off) % 16) * 2 + xh)

    def at_y(t):
        return (xl * 8 + ((y + y_order[t]) % 4) * 2 + co, h)

    def remote(src, dst, ss, rs, dev):
        return pltpu.make_async_remote_copy(
            src_ref=src, dst_ref=dst, send_sem=ss, recv_sem=rs, device_id=dev, device_id_type=MESH
        )

    def row_peer(off):
        j = (me + off) % 8
        return j, (((j // 2) % 2) * 8 + y * 2 + j % 2, z * 2 + j // 4)

    def quad_peer(off):
        q = (quad + off) % 4
        return q, ((q // 2) * 8 + y * 2 + q % 2, h)

    loads = [
        pltpu.make_async_copy(src, dst, in_sem.at[n])
        for n, (src, dst) in enumerate(
            [
                (r_any, r_ref),
                (p_any, p_ref),
                (pr_any, pr_ref),
                (pw_any, pw_ref),
                (rr_any, rr_ref),
                (cos_any, cos_ref),
                (aw_any, aw_ref),
                (cp_any, cp_ref),
            ]
        )
    ]
    for load in loads:
        load.start()

    barrier = pltpu.get_barrier_semaphore()

    @pl.loop(1, 16)
    def _(off):
        pl.semaphore_signal(barrier, inc=1, device_id=at_z(off), device_id_type=MESH)
        pl.semaphore_signal(barrier, inc=1, device_id=at_blk(off), device_id_type=MESH)

    @pl.loop(0, 4)
    def _(i):
        dev = ((i // 2) * 8 + y * 2 + i % 2, z * 2 + 1 - xh)
        pl.semaphore_signal(barrier, inc=1, device_id=dev, device_id_type=MESH)

    loads[0].wait()

    @pl.loop(0, 8)
    def _(n):
        t = r_ref[pl.ds(2 * n, 2)].reshape(128, 128).astype(F32).T
        lo, hi = t[:64], t[64:]
        for e, v in enumerate((lanes(lo[:, :64], hi[:, :64]), lanes(lo[:, 64:], hi[:, 64:]))):
            rows = pl.ds(pl.multiple_of((n % 2) * 32 + e * 16, 16), 16)
            for j in range(4):
                rz_send[j * 4 + n // 2, rows, :] = v[16 * j : 16 * j + 16].astype(BF16)

    pl.semaphore_wait(barrier, 34)

    @pl.loop(1, 16)
    def _(off):
        k = (z + off) % 16
        remote(rz_send.at[k], rz_got.at[z], rz_ss.at[off], rz_rs.at[z], at_z(off)).start()

    rz_got[z] = rz_send[z]

    loads[1].wait()

    @pl.loop(0, 16)
    def _(i):
        x = jnp.concatenate([p_ref[i], p_ref[16 + i]], axis=0)
        s_p[pl.ds(i, 128, stride=16), :] = x.astype(F32).T

    @pl.loop(0, 16)
    def _(off):
        d = (b + off) % 16
        for gh in range(2):
            for j in range(4):
                start = pl.multiple_of((gh * 64 + j * 16 + d) * 16, 16)
                p_send[d, gh, 16 * j : 16 * j + 16, :] = s_p[pl.ds(start, 16), :].astype(BF16)

        @pl.when(off > 0)
        def _():
            remote(p_send.at[d], p_got.at[b], pb_ss.at[off], pb_rs.at[b], at_blk(off)).start()

    p_got[b] = p_send[b]

    for load in loads[2:]:
        load.wait()
    for k in range(4):
        cols = slice(128 * k, 128 * k + 128)
        pr_t[cols, :] = jnp.broadcast_to(pr_ref[:, cols], (128, 128)).T
        pw_t[cols, :] = jnp.broadcast_to(pw_ref[:, cols], (128, 128)).T
    for k in range(2):
        cols = slice(128 * k, 128 * k + 128)
        rr_t[cols, :] = jnp.broadcast_to(rr_ref[:, cols], (128, 128)).T
    for qd in range(4):
        for i in range(4):
            near_t[pl.ds(qd * 64 + i, 16, stride=4), :] = rr_t[pl.ds(qd * 4 + i, 16, stride=16), :]
    for k in range(2):
        cols = slice(128 * k, 128 * k + 128)
        rr_t[cols, :] = near_t[cols, :].T

    @pl.loop(0, 8)
    def _(gi):
        g = (gi % 2) * 64 + (gi // 2) * 16 + b
        two_cos = 2.0 * cos_ref[0, g]
        ang = aw_ref[0, g]

        @pl.loop(0, 16)
        def _(src):
            for sh in range(2):
                rows = pl.ds(pl.multiple_of(src * 32 + sh * 16, 16), 16)
                far = pr_t[rows, :]
                scale = pw_t[rows, :] * ang
                far2 = far * far
                for half in range(2):
                    near = rr_t[128 * half : 128 * half + 16, :]
                    q = (1.0 + near * near) + far2 - (two_cos * near) * far
                    rs = lax.rsqrt(q)
                    root = q * rs
                    root = root + (0.5 * rs) * (q - root * root)
                    turns = root * turns_per_unit
                    f = turns - jnp.round(turns)
                    u = f * f
                    c = jnp.full_like(u, cos_terms[6])
                    for term in cos_terms[5::-1]:
                        c = c * u + term
                    w = scale * c * (rs * rs)
                    w_hi = w.astype(BF16)
                    w_lo = (w - w_hi.astype(F32)).astype(BF16)
                    at = pl.multiple_of(sh * 256 + src * 16, 16)
                    cols = slice(128 * half, 128 * half + 128)
                    weight[gi, pl.ds(at, 16), cols] = w_hi
                    weight[gi, pl.ds(at + 512, 16), cols] = w_lo

    @pl.loop(1, 16)
    def _(off):
        src = (b + off) % 16
        remote(p_send.at[0], p_got.at[src], pb_ss.at[0], pb_rs.at[src], at_blk(1)).wait_recv()

    def in_place(k):
        return in_got.at[k // 8, (k // 2) % 4, k % 2]

    def send_integral(k, e):
        rows = slice(32 * e, 32 * e + 32)

        @pl.when(k != z)
        def _():
            remote(
                in_send.at[k, rows], in_place(z).at[rows], iz_ss.at[e, k], iz_rs.at[e, z], (b, k * 2 + xh)
            ).start()

    @pl.loop(0, 4)
    def _(t):
        j = (z // 4 + 2 + t) % 4
        parts = []
        for gh in range(2):
            x = p_got[:, gh, pl.ds(pl.multiple_of(16 * j, 16), 16), :].reshape(256, 128)
            xt = x.T
            lhs = jnp.concatenate([xt[:64], xt[64:], xt[:64], xt[64:]], axis=1)
            parts.append(jnp.dot(lhs, weight[j * 2 + gh], preferred_element_type=F32))
        for qd in range(4):
            cols = slice(64 * qd, 64 * qd + 64)
            in_send[j * 4 + qd] = lanes(parts[0][:, cols], parts[1][:, cols]).astype(BF16)

        @pl.loop(0, 4)
        def _(qd):
            send_integral(j * 4 + qd, 0)

    @pl.loop(0, 16)
    def _(n):
        send_integral(((z // 4 + 2) * 4 + n) % 16, 1)

    in_got[z // 8, (z // 2) % 4, z % 2] = in_send[z]

    @pl.loop(0, 16)
    def _(off):
        src = (z + off) % 16

        @pl.when(off > 0)
        def _():
            remote(rz_send.at[0], rz_got.at[src], rz_ss.at[0], rz_rs.at[src], at_z(1)).wait_recv()

        v = rz_got[src].astype(F32)
        for i in range(4):
            s_r[pl.ds(16 * i + src, 16, stride=64), :] = v[16 * i : 16 * i + 16]

    @pl.loop(0, 16)
    def _(off):
        d = (b + off) % 16
        rb_send[d] = s_r[pl.ds(pl.multiple_of(64 * d, 64), 64), :].astype(BF16)

        @pl.when(off > 0)
        def _():
            remote(rb_send.at[d], rb_got.at[b], rb_ss.at[off], rb_rs.at[b], at_blk(off)).start()

    rb_got[b] = rb_send[b]

    @pl.loop(0, 16)
    def _(off):
        src = (b + off) % 16

        @pl.when(off > 0)
        def _():
            remote(rb_send.at[0], rb_got.at[src], rb_ss.at[0], rb_rs.at[src], at_blk(1)).wait_recv()

        s_r[pl.ds(pl.multiple_of(64 * src, 64), 64), :] = rb_got[src].astype(F32)

    @pl.loop(0, 16)
    def _(k):
        r_row[quad, k] = s_r[pl.ds(k, 64, stride=16), :].astype(BF16)

    @pl.loop(1, 4)
    def _(off):
        _, dev = quad_peer(off)
        remote(r_row.at[quad], r_row.at[quad], rr_ss.at[off], rr_rs.at[quad], dev).start()

    row_cols = pl.ds(pl.multiple_of(quad * 128, 128), 128)

    def integrals_to_row(e):
        rows = slice(32 * e, 32 * e + 32)

        @pl.loop(1, 16)
        def _(off):
            src = (z + off) % 16
            remote(
                in_send.at[0, rows], in_place(src).at[rows], iz_ss.at[e, 0], iz_rs.at[e, src], at_z(1)
            ).wait_recv()

        at = pl.ds(pl.multiple_of(xh * 32, 32), 32)

        @pl.loop(1, 8)
        def _(off):
            j, dev = row_peer(off)
            remote(
                in_got.at[(j // 2) % 2, :, j % 2, rows],
                in_row.at[e, :, at, row_cols],
                ir_ss.at[e, off],
                ir_rs.at[e, me],
                dev,
            ).start()

        in_row[e, :, at, row_cols] = in_got[xl, :, co, rows]

    integrals_to_row(0)

    @pl.loop(1, 4)
    def _(off):
        q, dev = quad_peer(off)
        remote(r_row.at[0], r_row.at[q], rr_ss.at[0], rr_rs.at[q], dev).wait_recv()

    @pl.loop(0, 4)
    def _(q):
        for n in range(8):
            x0 = r_row[q, 2 * n]
            x1 = r_row[q, 2 * n + 1]
            at = pl.multiple_of(q * 128, 128)
            cols = slice(128 * n, 128 * n + 128)
            rhs[pl.ds(at, 64), cols] = lanes(x0[:, :64], x1[:, :64])
            rhs[pl.ds(at + 64, 64), cols] = lanes(x0[:, 64:], x1[:, 64:])

    def share(e):
        @pl.loop(1, 8)
        def _(off):
            j, dev = row_peer(off)
            at = pl.ds(pl.multiple_of((j // 4) * 32, 32), 32)
            cols = pl.ds(pl.multiple_of((j % 4) * 128, 128), 128)
            remote(
                in_got.at[0, :, 0, 0:32], in_row.at[e, :, at, cols], ir_ss.at[e, 0], ir_rs.at[e, j], dev
            ).wait_recv()

        @pl.loop(0, 4)
        def _(n):
            cols = pl.ds(pl.multiple_of(n * 256, 256), 256)
            part = jnp.dot(in_row[e].reshape(256, 512), rhs[:, cols], preferred_element_type=F32)
            own[e, :, cols] = part
            y_send[e, :, :, cols] = part.astype(BF16).reshape(4, 64, 256)

        for t in range(3):
            yt = (y + y_order[t]) % 4
            remote(y_send.at[e, yt], y_got.at[e, t], y_ss.at[e, t], y_rs.at[e, t], at_y(t)).start()

    share(0)

    integrals_to_row(1)
    share(1)

    def plane_sum(e):
        for t in range(3):
            remote(y_send.at[e, 0], y_got.at[e, t], y_ss.at[e, t], y_rs.at[e, t], at_y(t)).wait_recv()

        @pl.loop(0, 8)
        def _(i):
            n = (z // 2 + 4 + i) % 8
            cols = pl.ds(pl.multiple_of(n * 128, 128), 128)
            s = own[e, pl.ds(pl.multiple_of(y * 64, 64), 64), cols]
            for t in range(3):
                s = s + y_got[e, t, :, cols].astype(F32)
            z_send[e, 2 * n] = lanes(s[:32, :64], s[32:, :64]).astype(BF16)
            z_send[e, 2 * n + 1] = lanes(s[:32, 64:], s[32:, 64:]).astype(BF16)

            @pl.loop(0, 2)
            def _(m):
                k = 2 * n + m

                @pl.when(k != z)
                def _():
                    remote(
                        z_send.at[e, k], z_got.at[e, z], z_ss.at[e, k], z_rs.at[e, z], (b, k * 2 + xh)
                    ).start()

                @pl.when(k == z)
                def _():
                    z_got[e, z] = z_send[e, z]

    plane_sum(0)
    plane_sum(1)

    totals = []
    for e in range(2):

        @pl.loop(1, 16)
        def _(off):
            src = (z + off) % 16
            remote(z_send.at[e, 0], z_got.at[e, src], z_ss.at[e, 0], z_rs.at[e, src], at_z(1)).wait_recv()

        total = z_got[e, 0].astype(F32)
        for k in range(1, 16):
            total = total + z_got[e, k].astype(F32)
        totals.append(total)
    out = jnp.concatenate(totals, axis=0).T
    o_ref[...] = lanes(out[:64] * cp_ref[0, 0].astype(F32), out[64:] * cp_ref[0, 1].astype(F32))

    @pl.loop(1, 16)
    def _(off):
        k = (z + off) % 16
        remote(rz_send.at[0], rz_got.at[0], rz_ss.at[off], rz_rs.at[0], at_z(1)).wait_send()
        remote(rb_send.at[0], rb_got.at[0], rb_ss.at[off], rb_rs.at[0], at_blk(1)).wait_send()
        remote(p_send.at[0], p_got.at[0], pb_ss.at[off], pb_rs.at[0], at_blk(1)).wait_send()
        for e in range(2):
            part = in_send.at[0, 0:32]
            remote(part, part, iz_ss.at[e, k], iz_rs.at[e, 0], at_z(1)).wait_send()
            remote(z_send.at[e, 0], z_got.at[e, 0], z_ss.at[e, k], z_rs.at[e, 0], at_z(1)).wait_send()

    @pl.loop(1, 4)
    def _(off):
        remote(r_row.at[0], r_row.at[0], rr_ss.at[off], rr_rs.at[0], at_blk(1)).wait_send()

    for e in range(2):

        @pl.loop(1, 8)
        def _(off):
            part = in_got.at[0, :, 0, 0:32]
            remote(part, part, ir_ss.at[e, off], ir_rs.at[e, 0], at_blk(1)).wait_send()

        for t in range(3):
            remote(y_send.at[e, 0], y_got.at[e, t], y_ss.at[e, t], y_rs.at[e, t], at_blk(1)).wait_send()


def local(react_basis, prod_basis, react_radius, prod_radius, prod_weight, angle_cos, angle_weight, coupling):
    dma = pltpu.SemaphoreType.DMA
    anywhere = pl.BlockSpec(memory_space=pl.ANY)
    full = pl.pallas_call(
        kernel,
        out_shape=jax.ShapeDtypeStruct((64, 128), F32),
        in_specs=[anywhere] * 8,
        out_specs=pl.BlockSpec(memory_space=pltpu.VMEM),
        scratch_shapes=[
            pltpu.VMEM((1, 512), F32),
            pltpu.VMEM((1, 512), F32),
            pltpu.VMEM((1, 256), F32),
            pltpu.SMEM((1, 128), F32),
            pltpu.SMEM((1, 128), F32),
            pltpu.SMEM((1, 2), jnp.int32),
            pltpu.VMEM((16, 64, 128), BF16),
            pltpu.VMEM((32, 64, 128), BF16),
            pltpu.VMEM((1024, 128), F32),
            pltpu.VMEM((2048, 128), F32),
            pltpu.VMEM((512, 128), F32),
            pltpu.VMEM((512, 128), F32),
            pltpu.VMEM((256, 128), F32),
            pltpu.VMEM((256, 128), F32),
            pltpu.VMEM((16, 64, 128), BF16),
            pltpu.VMEM((16, 64, 128), BF16),
            pltpu.VMEM((16, 64, 128), BF16),
            pltpu.VMEM((16, 64, 128), BF16),
            pltpu.VMEM((4, 16, 64, 128), BF16),
            pltpu.VMEM((512, 1024), BF16),
            pltpu.VMEM((16, 2, 64, 128), BF16),
            pltpu.VMEM((16, 2, 64, 128), BF16),
            pltpu.VMEM((8, 1024, 256), BF16),
            pltpu.VMEM((16, 64, 128), BF16),
            pltpu.VMEM((2, 4, 2, 64, 128), BF16),
            pltpu.VMEM((2, 4, 64, 512), BF16),
            pltpu.VMEM((2, 4, 64, 1024), BF16),
            pltpu.VMEM((2, 3, 64, 1024), BF16),
            pltpu.VMEM((2, 256, 1024), F32),
            pltpu.VMEM((2, 16, 32, 128), BF16),
            pltpu.VMEM((2, 16, 32, 128), BF16),
            dma((8,)),
            dma((16,)),
            dma((16,)),
            dma((16,)),
            dma((16,)),
            dma((4,)),
            dma((4,)),
            dma((16,)),
            dma((16,)),
            dma((2, 16)),
            dma((2, 16)),
            dma((2, 8)),
            dma((2, 8)),
            dma((2, 3)),
            dma((2, 3)),
            dma((2, 16)),
            dma((2, 16)),
        ],
        compiler_params=pltpu.CompilerParams(
            collective_id=0, has_side_effects=True, vmem_limit_bytes=60 * 2**20
        ),
        cost_estimate=pl.CostEstimate(flops=10**9, bytes_accessed=10**6, transcendentals=10**6),
    )(
        prod_radius.reshape(1, -1),
        prod_weight.reshape(1, -1),
        react_radius.reshape(1, -1),
        angle_cos.reshape(1, -1),
        angle_weight.reshape(1, -1),
        coupling.reshape(1, -1),
        react_basis,
        prod_basis,
    )
    return full.T


def solution(mesh):
    return jax.shard_map(
        local,
        mesh=mesh,
        in_specs=(P("blk", "chan", None), P("blk", "chan", None), P(), P(), P(), P(), P(), P("blk", "chan")),
        out_specs=P("blk", "chan"),
        check_vma=False,
    )
```

time: 93.2 us -> 84.7 us (0.909)
  the two profiles are of different devices: /device:TPU:8 before, /device:TPU:1 now
where the time goes in v2:
time: 84.7 us; the launch traced here: 84.6 us
  Pallas kernels  83.2 us (98%)
  local copies, waits for them, and re-layouts  1.38 us (2%)
    pallas_call x1, Pallas kernels, local(): pl.pallas_call(kernel, out_shape=jax.ShapeDtypeStruct((64, 128), F32), in...  83.2 us

profile of v2, /device:TPU:1, one launch (start us, length us, event | category | flops | bytes accessed | tf_op | source)
XLA Modules:
  0.0 84.6 jit_solution(2567880420851791823)
XLA Ops:
  0.0 83.2 %shard_map.82 = f32[64,128]{1,0:T(8,128)} custom-call(f32[1,512]{1,0:T(1,128)} %bitcast.8, f32[1,512]{1,0:T(1,128)} %bitcast.9, f32[1,256]{1,0:T(1,128)} %bitcast.10, f32[1,128]{1,0:T(1,128)} %bitcast.11, f32[1,128]{1,0:T(1,128)} %bitcast.12, s32[1,2]{1,0:T(1,128)} %bitcast.13, bf16[16,64,128]{2,1,0:T(8,128)(2,1)} %r_any.1, bf16[32,64,128]{2,1,0:T(8,128)(2,1)} %p_any.1), custom_call_target="tpu_custom_call" | custom-call | flops 1000000000 | bytes 1000000 | tf_op jit(solution)/shard_map/pallas_call | solution.py:464
  83.2 1.4 %copy.10 = f32[128,64]{0,1:T(8,128)} copy(f32[128,64]{0,1:T(8,128)} %bitcast.7) | data formatting | bytes 65536

commit v3 on v2

--- a/solution.py
+++ b/solution.py
@@ -20,6 +20,8 @@
     6.528658162567069,
 )
 y_order = (2, 1, 3)
+parts = 4
+depth = 64 // parts
 
 
 def lanes(a, b):
@@ -52,8 +54,6 @@
     near_t,
     rz_send,
     rz_got,
-    rb_send,
-    rb_got,
     r_row,
     rhs,
     p_send,
@@ -72,8 +72,8 @@
     rz_rs,
     rb_ss,
     rb_rs,
-    rr_ss,
-    rr_rs,
+    rc_ss,
+    rc_rs,
     pb_ss,
     pb_rs,
     iz_ss,
@@ -110,10 +110,6 @@
         j = (me + off) % 8
         return j, (((j // 2) % 2) * 8 + y * 2 + j % 2, z * 2 + j // 4)
 
-    def quad_peer(off):
-        q = (quad + off) % 4
-        return q, ((q // 2) * 8 + y * 2 + q % 2, h)
-
     loads = [
         pltpu.make_async_copy(src, dst, in_sem.at[n])
         for n, (src, dst) in enumerate(
@@ -150,19 +146,32 @@
     def _(n):
         t = r_ref[pl.ds(2 * n, 2)].reshape(128, 128).astype(F32).T
         lo, hi = t[:64], t[64:]
-        for e, v in enumerate((lanes(lo[:, :64], hi[:, :64]), lanes(lo[:, 64:], hi[:, 64:]))):
-            rows = pl.ds(pl.multiple_of((n % 2) * 32 + e * 16, 16), 16)
-            for j in range(4):
-                rz_send[j * 4 + n // 2, rows, :] = v[16 * j : 16 * j + 16].astype(BF16)
+        s_r[pl.ds(2 * n, 64, stride=16), :] = lanes(lo[:, :64], hi[:, :64])
+        s_r[pl.ds(2 * n + 1, 64, stride=16), :] = lanes(lo[:, 64:], hi[:, 64:])
+
+    for e in range(2):
+        for j in range(8):
+            at = j * 128 + e * 64
+            rz_send[e, j] = s_r[at : at + 64, :].astype(BF16).reshape(4, 16, 128)
 
     pl.semaphore_wait(barrier, 34)
 
-    @pl.loop(1, 16)
-    def _(off):
-        k = (z + off) % 16
-        remote(rz_send.at[k], rz_got.at[z], rz_ss.at[off], rz_rs.at[z], at_z(off)).start()
-
-    rz_got[z] = rz_send[z]
+    for e in range(2):
+
+        @pl.loop(0, 8)
+        def _(off):
+            j = (z // 2 + off) % 8
+            k = j * 2 + co
+
+            @pl.when(k != z)
+            def _():
+                remote(
+                    rz_send.at[e, j], rz_got.at[e, z], rz_ss.at[e, j], rz_rs.at[e, z], (b, k * 2 + xh)
+                ).start()
+
+            @pl.when(k == z)
+            def _():
+                rz_got[e, z] = rz_send[e, j]
 
     loads[1].wait()
 
@@ -174,10 +183,9 @@
     @pl.loop(0, 16)
     def _(off):
         d = (b + off) % 16
-        for gh in range(2):
-            for j in range(4):
-                start = pl.multiple_of((gh * 64 + j * 16 + d) * 16, 16)
-                p_send[d, gh, 16 * j : 16 * j + 16, :] = s_p[pl.ds(start, 16), :].astype(BF16)
+        for j in range(8):
+            start = pl.multiple_of(((d % 2) * 64 + j * 8 + d // 2) * 16, 16)
+            p_send[d, 16 * j : 16 * j + 16, :] = s_p[pl.ds(start, 16), :].astype(BF16)
 
         @pl.when(off > 0)
         def _():
@@ -194,16 +202,16 @@
     for k in range(2):
         cols = slice(128 * k, 128 * k + 128)
         rr_t[cols, :] = jnp.broadcast_to(rr_ref[:, cols], (128, 128)).T
-    for qd in range(4):
-        for i in range(4):
-            near_t[pl.ds(qd * 64 + i, 16, stride=4), :] = rr_t[pl.ds(qd * 4 + i, 16, stride=16), :]
+    for k in range(16):
+        at = (k % 2) * 128 + (k // 2) * 16
+        near_t[at : at + 16, :] = rr_t[16 * k : 16 * k + 16, :]
     for k in range(2):
         cols = slice(128 * k, 128 * k + 128)
         rr_t[cols, :] = near_t[cols, :].T
 
     @pl.loop(0, 8)
     def _(gi):
-        g = (gi % 2) * 64 + (gi // 2) * 16 + b
+        g = co * 64 + gi * 8 + b // 2
         two_cos = 2.0 * cos_ref[0, g]
         ang = aw_ref[0, g]
 
@@ -234,6 +242,51 @@
                     weight[gi, pl.ds(at, 16), cols] = w_hi
                     weight[gi, pl.ds(at + 512, 16), cols] = w_lo
 
+    holder = co == z % 2
+
+    def react_to_rows(e):
+        @pl.when(holder)
+        def _():
+            @pl.loop(1, 16)
+            def _(off):
+                src = (z + off) % 16
+                remote(
+                    rz_send.at[e, 0], rz_got.at[e, src], rz_ss.at[e, 0], rz_rs.at[e, src], at_z(1)
+                ).wait_recv()
+
+            rows = pl.ds(pl.multiple_of((b // 2) * 16, 16), 16)
+
+            @pl.loop(1, 8)
+            def _(off):
+                d = (b + 2 * off) % 16
+                remote(
+                    rz_got.at[e, :, (d // 2) % 4],
+                    r_row.at[e, :, rows],
+                    rb_ss.at[e, off],
+                    rb_rs.at[e, b // 2],
+                    at_blk(2 * off),
+                ).start()
+
+            r_row[e, :, rows] = rz_got[e, :, y]
+
+    def other_core():
+        return (b + 1 - 2 * co, h)
+
+    def react_to_core(e):
+        @pl.when(holder)
+        def _():
+            @pl.loop(1, 8)
+            def _(off):
+                n = (b // 2 + off) % 8
+                rows = pl.ds(pl.multiple_of(n * 16, 16), 16)
+                remote(
+                    rz_got.at[e, :, 0], r_row.at[e, :, rows], rb_ss.at[e, 0], rb_rs.at[e, n], at_blk(2)
+                ).wait_recv()
+
+            remote(r_row.at[e], r_row.at[e], rc_ss.at[e], rc_rs.at[e], other_core()).start()
+
+    react_to_rows(0)
+
     @pl.loop(1, 16)
     def _(off):
         src = (b + off) % 16
@@ -243,7 +296,7 @@
         return in_got.at[k // 8, (k // 2) % 4, k % 2]
 
     def send_integral(k, e):
-        rows = slice(32 * e, 32 * e + 32)
+        rows = slice(depth * e, depth * e + depth)
 
         @pl.when(k != z)
         def _():
@@ -251,75 +304,32 @@
                 in_send.at[k, rows], in_place(z).at[rows], iz_ss.at[e, k], iz_rs.at[e, z], (b, k * 2 + xh)
             ).start()
 
-    @pl.loop(0, 4)
+    @pl.loop(0, 8)
     def _(t):
-        j = (z // 4 + 2 + t) % 4
-        parts = []
-        for gh in range(2):
-            x = p_got[:, gh, pl.ds(pl.multiple_of(16 * j, 16), 16), :].reshape(256, 128)
-            xt = x.T
-            lhs = jnp.concatenate([xt[:64], xt[64:], xt[:64], xt[64:]], axis=1)
-            parts.append(jnp.dot(lhs, weight[j * 2 + gh], preferred_element_type=F32))
-        for qd in range(4):
-            cols = slice(64 * qd, 64 * qd + 64)
-            in_send[j * 4 + qd] = lanes(parts[0][:, cols], parts[1][:, cols]).astype(BF16)
-
-        @pl.loop(0, 4)
-        def _(qd):
-            send_integral(j * 4 + qd, 0)
-
-    @pl.loop(0, 16)
-    def _(n):
-        send_integral(((z // 4 + 2) * 4 + n) % 16, 1)
+        j = (z // 2 + 4 + t) % 8
+        x = p_got[:, pl.ds(pl.multiple_of(16 * j, 16), 16), :].reshape(256, 128)
+        xt = x.T
+        lhs = jnp.concatenate([xt[:64], xt[64:], xt[:64], xt[64:]], axis=1)
+        part = jnp.dot(lhs, weight[j], preferred_element_type=F32)
+        for n in range(2):
+            in_send[j * 2 + n] = part[:, 128 * n : 128 * n + 128].astype(BF16)
+            send_integral(j * 2 + n, 0)
+
+    for e in range(1, parts):
+
+        @pl.loop(0, 16)
+        def _(n):
+            send_integral(((z // 2 + 4) * 2 + n) % 16, e)
 
     in_got[z // 8, (z // 2) % 4, z % 2] = in_send[z]
 
-    @pl.loop(0, 16)
-    def _(off):
-        src = (z + off) % 16
-
-        @pl.when(off > 0)
-        def _():
-            remote(rz_send.at[0], rz_got.at[src], rz_ss.at[0], rz_rs.at[src], at_z(1)).wait_recv()
-
-        v = rz_got[src].astype(F32)
-        for i in range(4):
-            s_r[pl.ds(16 * i + src, 16, stride=64), :] = v[16 * i : 16 * i + 16]
-
-    @pl.loop(0, 16)
-    def _(off):
-        d = (b + off) % 16
-        rb_send[d] = s_r[pl.ds(pl.multiple_of(64 * d, 64), 64), :].astype(BF16)
-
-        @pl.when(off > 0)
-        def _():
-            remote(rb_send.at[d], rb_got.at[b], rb_ss.at[off], rb_rs.at[b], at_blk(off)).start()
-
-    rb_got[b] = rb_send[b]
-
-    @pl.loop(0, 16)
-    def _(off):
-        src = (b + off) % 16
-
-        @pl.when(off > 0)
-        def _():
-            remote(rb_send.at[0], rb_got.at[src], rb_ss.at[0], rb_rs.at[src], at_blk(1)).wait_recv()
-
-        s_r[pl.ds(pl.multiple_of(64 * src, 64), 64), :] = rb_got[src].astype(F32)
-
-    @pl.loop(0, 16)
-    def _(k):
-        r_row[quad, k] = s_r[pl.ds(k, 64, stride=16), :].astype(BF16)
-
-    @pl.loop(1, 4)
-    def _(off):
-        _, dev = quad_peer(off)
-        remote(r_row.at[quad], r_row.at[quad], rr_ss.at[off], rr_rs.at[quad], dev).start()
+    react_to_rows(1)
+    react_to_core(0)
 
     row_cols = pl.ds(pl.multiple_of(quad * 128, 128), 128)
 
     def integrals_to_row(e):
-        rows = slice(32 * e, 32 * e + 32)
+        rows = slice(depth * e, depth * e + depth)
 
         @pl.loop(1, 16)
         def _(off):
@@ -328,7 +338,7 @@
                 in_send.at[0, rows], in_place(src).at[rows], iz_ss.at[e, 0], iz_rs.at[e, src], at_z(1)
             ).wait_recv()
 
-        at = pl.ds(pl.multiple_of(xh * 32, 32), 32)
+        at = pl.ds(pl.multiple_of(xh * depth, depth), depth)
 
         @pl.loop(1, 8)
         def _(off):
@@ -344,47 +354,42 @@
         in_row[e, :, at, row_cols] = in_got[xl, :, co, rows]
 
     integrals_to_row(0)
-
-    @pl.loop(1, 4)
-    def _(off):
-        q, dev = quad_peer(off)
-        remote(r_row.at[0], r_row.at[q], rr_ss.at[0], rr_rs.at[q], dev).wait_recv()
-
-    @pl.loop(0, 4)
-    def _(q):
-        for n in range(8):
-            x0 = r_row[q, 2 * n]
-            x1 = r_row[q, 2 * n + 1]
-            at = pl.multiple_of(q * 128, 128)
-            cols = slice(128 * n, 128 * n + 128)
-            rhs[pl.ds(at, 64), cols] = lanes(x0[:, :64], x1[:, :64])
-            rhs[pl.ds(at + 64, 64), cols] = lanes(x0[:, 64:], x1[:, 64:])
+    react_to_core(1)
+
+    for e in range(2):
+
+        @pl.when(jnp.logical_not(holder))
+        def _():
+            remote(r_row.at[e], r_row.at[e], rc_ss.at[e], rc_rs.at[e], other_core()).wait_recv()
+
+        @pl.loop(0, 8)
+        def _(n):
+            x0 = r_row[e, 2 * n]
+            x1 = r_row[e, 2 * n + 1]
+            cols = pl.ds(pl.multiple_of(n * 128, 128), 128)
+            rhs[256 * e : 256 * e + 128, cols] = lanes(x0[:, :64], x1[:, :64])
+            rhs[256 * e + 128 : 256 * e + 256, cols] = lanes(x0[:, 64:], x1[:, 64:])
 
     def share(e):
         @pl.loop(1, 8)
         def _(off):
             j, dev = row_peer(off)
-            at = pl.ds(pl.multiple_of((j // 4) * 32, 32), 32)
+            at = pl.ds(pl.multiple_of((j // 4) * depth, depth), depth)
             cols = pl.ds(pl.multiple_of((j % 4) * 128, 128), 128)
             remote(
-                in_got.at[0, :, 0, 0:32], in_row.at[e, :, at, cols], ir_ss.at[e, 0], ir_rs.at[e, j], dev
+                in_got.at[0, :, 0, 0:depth], in_row.at[e, :, at, cols], ir_ss.at[e, 0], ir_rs.at[e, j], dev
             ).wait_recv()
 
         @pl.loop(0, 4)
         def _(n):
             cols = pl.ds(pl.multiple_of(n * 256, 256), 256)
-            part = jnp.dot(in_row[e].reshape(256, 512), rhs[:, cols], preferred_element_type=F32)
+            part = jnp.dot(in_row[e].reshape(8 * depth, 512), rhs[:, cols], preferred_element_type=F32)
             own[e, :, cols] = part
-            y_send[e, :, :, cols] = part.astype(BF16).reshape(4, 64, 256)
+            y_send[e, :, :, cols] = part.astype(BF16).reshape(4, 2 * depth, 256)
 
         for t in range(3):
             yt = (y + y_order[t]) % 4
             remote(y_send.at[e, yt], y_got.at[e, t], y_ss.at[e, t], y_rs.at[e, t], at_y(t)).start()
-
-    share(0)
-
-    integrals_to_row(1)
-    share(1)
 
     def plane_sum(e):
         for t in range(3):
@@ -394,11 +399,11 @@
         def _(i):
             n = (z // 2 + 4 + i) % 8
             cols = pl.ds(pl.multiple_of(n * 128, 128), 128)
-            s = own[e, pl.ds(pl.multiple_of(y * 64, 64), 64), cols]
+            s = own[e, pl.ds(pl.multiple_of(y * (2 * depth), 2 * depth), 2 * depth), cols]
             for t in range(3):
                 s = s + y_got[e, t, :, cols].astype(F32)
-            z_send[e, 2 * n] = lanes(s[:32, :64], s[32:, :64]).astype(BF16)
-            z_send[e, 2 * n + 1] = lanes(s[:32, 64:], s[32:, 64:]).astype(BF16)
+            z_send[e, 2 * n] = lanes(s[:depth, :64], s[depth:, :64]).astype(BF16)
+            z_send[e, 2 * n + 1] = lanes(s[:depth, 64:], s[depth:, 64:]).astype(BF16)
 
             @pl.loop(0, 2)
             def _(m):
@@ -414,11 +419,16 @@
                 def _():
                     z_got[e, z] = z_send[e, z]
 
-    plane_sum(0)
-    plane_sum(1)
+    for n in range(1, parts + 2):
+        if n < parts:
+            integrals_to_row(n)
+        if n <= parts:
+            share(n - 1)
+        if n >= 2:
+            plane_sum(n - 2)
 
     totals = []
-    for e in range(2):
+    for e in range(parts):
 
         @pl.loop(1, 16)
         def _(off):
@@ -435,23 +445,34 @@
     @pl.loop(1, 16)
     def _(off):
         k = (z + off) % 16
-        remote(rz_send.at[0], rz_got.at[0], rz_ss.at[off], rz_rs.at[0], at_z(1)).wait_send()
-        remote(rb_send.at[0], rb_got.at[0], rb_ss.at[off], rb_rs.at[0], at_blk(1)).wait_send()
         remote(p_send.at[0], p_got.at[0], pb_ss.at[off], pb_rs.at[0], at_blk(1)).wait_send()
-        for e in range(2):
-            part = in_send.at[0, 0:32]
+        for e in range(parts):
+            part = in_send.at[0, 0:depth]
             remote(part, part, iz_ss.at[e, k], iz_rs.at[e, 0], at_z(1)).wait_send()
             remote(z_send.at[e, 0], z_got.at[e, 0], z_ss.at[e, k], z_rs.at[e, 0], at_z(1)).wait_send()
 
-    @pl.loop(1, 4)
-    def _(off):
-        remote(r_row.at[0], r_row.at[0], rr_ss.at[off], rr_rs.at[0], at_blk(1)).wait_send()
-
     for e in range(2):
+
+        @pl.loop(0, 8)
+        def _(j):
+            @pl.when(j * 2 + co != z)
+            def _():
+                remote(rz_send.at[e, j], rz_send.at[e, j], rz_ss.at[e, j], rz_rs.at[e, 0], at_z(1)).wait_send()
+
+        @pl.when(holder)
+        def _():
+            @pl.loop(1, 8)
+            def _(off):
+                some = rz_got.at[e, :, 0]
+                remote(some, some, rb_ss.at[e, off], rb_rs.at[e, 0], at_blk(1)).wait_send()
+
+            remote(r_row.at[e], r_row.at[e], rc_ss.at[e], rc_rs.at[e], other_core()).wait_send()
+
+    for e in range(parts):
 
         @pl.loop(1, 8)
         def _(off):
-            part = in_got.at[0, :, 0, 0:32]
+            part = in_got.at[0, :, 0, 0:depth]
             remote(part, part, ir_ss.at[e, off], ir_rs.at[e, 0], at_blk(1)).wait_send()
 
         for t in range(3):
@@ -481,40 +502,38 @@
             pltpu.VMEM((512, 128), F32),
             pltpu.VMEM((256, 128), F32),
             pltpu.VMEM((256, 128), F32),
-            pltpu.VMEM((16, 64, 128), BF16),
-            pltpu.VMEM((16, 64, 128), BF16),
-            pltpu.VMEM((16, 64, 128), BF16),
-            pltpu.VMEM((16, 64, 128), BF16),
-            pltpu.VMEM((4, 16, 64, 128), BF16),
+            pltpu.VMEM((2, 8, 4, 16, 128), BF16),
+            pltpu.VMEM((2, 16, 4, 16, 128), BF16),
+            pltpu.VMEM((2, 16, 128, 128), BF16),
             pltpu.VMEM((512, 1024), BF16),
-            pltpu.VMEM((16, 2, 64, 128), BF16),
-            pltpu.VMEM((16, 2, 64, 128), BF16),
+            pltpu.VMEM((16, 128, 128), BF16),
+            pltpu.VMEM((16, 128, 128), BF16),
             pltpu.VMEM((8, 1024, 256), BF16),
             pltpu.VMEM((16, 64, 128), BF16),
             pltpu.VMEM((2, 4, 2, 64, 128), BF16),
-            pltpu.VMEM((2, 4, 64, 512), BF16),
-            pltpu.VMEM((2, 4, 64, 1024), BF16),
-            pltpu.VMEM((2, 3, 64, 1024), BF16),
-            pltpu.VMEM((2, 256, 1024), F32),
-            pltpu.VMEM((2, 16, 32, 128), BF16),
-            pltpu.VMEM((2, 16, 32, 128), BF16),
+            pltpu.VMEM((parts, 4, 2 * depth, 512), BF16),
+            pltpu.VMEM((parts, 4, 2 * depth, 1024), BF16),
+            pltpu.VMEM((parts, 3, 2 * depth, 1024), BF16),
+            pltpu.VMEM((parts, 8 * depth, 1024), F32),
+            pltpu.VMEM((parts, 16, depth, 128), BF16),
+            pltpu.VMEM((parts, 16, depth, 128), BF16),
             dma((8,)),
-            dma((16,)),
-            dma((16,)),
-            dma((16,)),
-            dma((16,)),
-            dma((4,)),
-            dma((4,)),
-            dma((16,)),
-            dma((16,)),
-            dma((2, 16)),
+            dma((2, 8)),
             dma((2, 16)),
             dma((2, 8)),
             dma((2, 8)),
-            dma((2, 3)),
-            dma((2, 3)),
-            dma((2, 16)),
-            dma((2, 16)),
+            dma((2,)),
+            dma((2,)),
+            dma((16,)),
+            dma((16,)),
+            dma((parts, 16)),
+            dma((parts, 16)),
+            dma((parts, 8)),
+            dma((parts, 8)),
+            dma((parts, 3)),
+            dma((parts, 3)),
+            dma((parts, 16)),
+            dma((parts, 16)),
         ],
         compiler_params=pltpu.CompilerParams(
             collective_id=0, has_side_effects=True, vmem_limit_bytes=60 * 2**20

time: 84.7 us -> 75.3 us (0.89)
  Pallas kernels: 83.2 us -> 73.7 us
    pallas_call x1, Pallas kernels: 83.2 us -> 73.7 us  [local(): pl.pallas_call(kernel, out_shape=jax.ShapeDtypeStruct((64, 128), F32), in...]
where the time goes in v3:
time: 75.3 us; the launch traced here: 75.1 us
  Pallas kernels  73.7 us (98%)
  local copies, waits for them, and re-layouts  1.38 us (2%)
    pallas_call x1, Pallas kernels, local(): pl.pallas_call(kernel, out_shape=jax.ShapeDtypeStruct((64, 128), F32), in...  73.7 us

profile of v3, /device:TPU:1, one launch (start us, length us, event | category | flops | bytes accessed | tf_op | source)
XLA Modules:
  0.0 75.1 jit_solution(10962478775939132383)
XLA Ops:
  0.0 73.7 %shard_map.82 = f32[64,128]{1,0:T(8,128)} custom-call(f32[1,512]{1,0:T(1,128)} %bitcast.8, f32[1,512]{1,0:T(1,128)} %bitcast.9, f32[1,256]{1,0:T(1,128)} %bitcast.10, f32[1,128]{1,0:T(1,128)} %bitcast.11, f32[1,128]{1,0:T(1,128)} %bitcast.12, s32[1,2]{1,0:T(1,128)} %bitcast.13, bf16[16,64,128]{2,1,0:T(8,128)(2,1)} %r_any.1, bf16[32,64,128]{2,1,0:T(8,128)(2,1)} %p_any.1), custom_call_target="tpu_custom_call" | custom-call | flops 1000000000 | bytes 1000000 | tf_op jit(solution)/shard_map/pallas_call | solution.py:485
  73.7 1.4 %copy.10 = f32[128,64]{0,1:T(8,128)} copy(f32[128,64]{0,1:T(8,128)} %bitcast.7) | data formatting | bytes 65536

commit v4 on v3

--- a/solution.py
+++ b/solution.py
@@ -22,6 +22,10 @@
 y_order = (2, 1, 3)
 parts = 4
 depth = 64 // parts
+
+
+def far_first(half, t):
+    return half + (1 - 2 * (t % 2)) * ((t + 1) // 2)
 
 
 def lanes(a, b):
@@ -160,7 +164,7 @@
 
         @pl.loop(0, 8)
         def _(off):
-            j = (z // 2 + off) % 8
+            j = (z // 2 + far_first(4, off)) % 8
             k = j * 2 + co
 
             @pl.when(k != z)
@@ -304,9 +308,9 @@
                 in_send.at[k, rows], in_place(z).at[rows], iz_ss.at[e, k], iz_rs.at[e, z], (b, k * 2 + xh)
             ).start()
 
-    @pl.loop(0, 8)
+    @pl.loop(0, 8, unroll=2)
     def _(t):
-        j = (z // 2 + 4 + t) % 8
+        j = (z // 2 + far_first(4, t)) % 8
         x = p_got[:, pl.ds(pl.multiple_of(16 * j, 16), 16), :].reshape(256, 128)
         xt = x.T
         lhs = jnp.concatenate([xt[:64], xt[64:], xt[:64], xt[64:]], axis=1)
@@ -317,9 +321,14 @@
 
     for e in range(1, parts):
 
-        @pl.loop(0, 16)
-        def _(n):
-            send_integral(((z // 2 + 4) * 2 + n) % 16, e)
+        @pl.loop(0, 15)
+        def _(t):
+            off = far_first(8, t)
+            k = (z + off) % 16
+            rows = slice(depth * e, depth * e + depth)
+            remote(
+                in_send.at[k, rows], in_place(z).at[rows], iz_ss.at[e, k], iz_rs.at[e, z], at_z(off)
+            ).start()
 
     in_got[z // 8, (z // 2) % 4, z % 2] = in_send[z]
 
@@ -380,9 +389,8 @@
                 in_got.at[0, :, 0, 0:depth], in_row.at[e, :, at, cols], ir_ss.at[e, 0], ir_rs.at[e, j], dev
             ).wait_recv()
 
-        @pl.loop(0, 4)
-        def _(n):
-            cols = pl.ds(pl.multiple_of(n * 256, 256), 256)
+        for n in range(4):
+            cols = slice(256 * n, 256 * n + 256)
             part = jnp.dot(in_row[e].reshape(8 * depth, 512), rhs[:, cols], preferred_element_type=F32)
             own[e, :, cols] = part
             y_send[e, :, :, cols] = part.astype(BF16).reshape(4, 2 * depth, 256)
@@ -395,29 +403,22 @@
         for t in range(3):
             remote(y_send.at[e, 0], y_got.at[e, t], y_ss.at[e, t], y_rs.at[e, t], at_y(t)).wait_recv()
 
-        @pl.loop(0, 8)
-        def _(i):
-            n = (z // 2 + 4 + i) % 8
-            cols = pl.ds(pl.multiple_of(n * 128, 128), 128)
-            s = own[e, pl.ds(pl.multiple_of(y * (2 * depth), 2 * depth), 2 * depth), cols]
+        mine = pl.ds(pl.multiple_of(y * (2 * depth), 2 * depth), 2 * depth)
+        for n in range(8):
+            cols = slice(128 * n, 128 * n + 128)
+            s = own[e, mine, cols]
             for t in range(3):
                 s = s + y_got[e, t, :, cols].astype(F32)
             z_send[e, 2 * n] = lanes(s[:depth, :64], s[depth:, :64]).astype(BF16)
             z_send[e, 2 * n + 1] = lanes(s[:depth, 64:], s[depth:, 64:]).astype(BF16)
 
-            @pl.loop(0, 2)
-            def _(m):
-                k = 2 * n + m
-
-                @pl.when(k != z)
-                def _():
-                    remote(
-                        z_send.at[e, k], z_got.at[e, z], z_ss.at[e, k], z_rs.at[e, z], (b, k * 2 + xh)
-                    ).start()
-
-                @pl.when(k == z)
-                def _():
-                    z_got[e, z] = z_send[e, z]
+        @pl.loop(0, 15)
+        def _(t):
+            off = far_first(8, t)
+            k = (z + off) % 16
+            remote(z_send.at[e, k], z_got.at[e, z], z_ss.at[e, off], z_rs.at[e, z], at_z(off)).start()
+
+        z_got[e, z] = z_send[e, z]
 
     for n in range(1, parts + 2):
         if n < parts:
@@ -427,21 +428,6 @@
         if n >= 2:
             plane_sum(n - 2)
 
-    totals = []
-    for e in range(parts):
-
-        @pl.loop(1, 16)
-        def _(off):
-            src = (z + off) % 16
-            remote(z_send.at[e, 0], z_got.at[e, src], z_ss.at[e, 0], z_rs.at[e, src], at_z(1)).wait_recv()
-
-        total = z_got[e, 0].astype(F32)
-        for k in range(1, 16):
-            total = total + z_got[e, k].astype(F32)
-        totals.append(total)
-    out = jnp.concatenate(totals, axis=0).T
-    o_ref[...] = lanes(out[:64] * cp_ref[0, 0].astype(F32), out[64:] * cp_ref[0, 1].astype(F32))
-
     @pl.loop(1, 16)
     def _(off):
         k = (z + off) % 16
@@ -449,7 +435,6 @@
         for e in range(parts):
             part = in_send.at[0, 0:depth]
             remote(part, part, iz_ss.at[e, k], iz_rs.at[e, 0], at_z(1)).wait_send()
-            remote(z_send.at[e, 0], z_got.at[e, 0], z_ss.at[e, k], z_rs.at[e, 0], at_z(1)).wait_send()
 
     for e in range(2):
 
@@ -477,6 +462,21 @@
 
         for t in range(3):
             remote(y_send.at[e, 0], y_got.at[e, t], y_ss.at[e, t], y_rs.at[e, t], at_blk(1)).wait_send()
+
+    totals = []
+    for e in range(parts):
+
+        @pl.loop(1, 16)
+        def _(off):
+            src = (z + off) % 16
+            remote(z_send.at[e, 0], z_got.at[e, src], z_ss.at[e, off], z_rs.at[e, src], at_z(1)).wait()
+
+        total = z_got[e, 0].astype(F32)
+        for k in range(1, 16):
+            total = total + z_got[e, k].astype(F32)
+        totals.append(total)
+    out = jnp.concatenate(totals, axis=0).T
+    o_ref[...] = lanes(out[:64] * cp_ref[0, 0].astype(F32), out[64:] * cp_ref[0, 1].astype(F32))
 
 
 def local(react_basis, prod_basis, react_radius, prod_radius, prod_weight, angle_cos, angle_weight, coupling):

time: 75.3 us -> 71 us (0.943)
  Pallas kernels: 73.7 us -> 69.4 us
    pallas_call x1, Pallas kernels: 73.7 us -> 69.4 us  [local(): pl.pallas_call(kernel, out_shape=jax.ShapeDtypeStruct((64, 128), F32), in...]
where the time goes in v4:
time: 71 us; the launch traced here: 70.8 us
  Pallas kernels  69.4 us (98%)
  local copies, waits for them, and re-layouts  1.38 us (2%)
    pallas_call x1, Pallas kernels, local(): pl.pallas_call(kernel, out_shape=jax.ShapeDtypeStruct((64, 128), F32), in...  69.4 us

profile of v4, /device:TPU:1, one launch (start us, length us, event | category | flops | bytes accessed | tf_op | source)
XLA Modules:
  0.0 70.8 jit_solution(16444080626914167176)
XLA Ops:
  0.0 69.4 %shard_map.82 = f32[64,128]{1,0:T(8,128)} custom-call(f32[1,512]{1,0:T(1,128)} %bitcast.8, f32[1,512]{1,0:T(1,128)} %bitcast.9, f32[1,256]{1,0:T(1,128)} %bitcast.10, f32[1,128]{1,0:T(1,128)} %bitcast.11, f32[1,128]{1,0:T(1,128)} %bitcast.12, s32[1,2]{1,0:T(1,128)} %bitcast.13, bf16[16,64,128]{2,1,0:T(8,128)(2,1)} %r_any.1, bf16[32,64,128]{2,1,0:T(8,128)(2,1)} %p_any.1), custom_call_target="tpu_custom_call" | custom-call | flops 1000000000 | bytes 1000000 | tf_op jit(solution)/shard_map/pallas_call | solution.py:485
  69.4 1.4 %copy.10 = f32[128,64]{0,1:T(8,128)} copy(f32[128,64]{0,1:T(8,128)} %bitcast.7) | data formatting | bytes 65536
